TPU v7x, 32 devices: a whole 2x2x4 slice. The times are simulated.
32 devices in a mesh: rep: 4 (over z), fsdp: 8 (over y, x, core).
Axes of the slice: x: 2, y: 2, z: 4, core: 2. Of those that a mesh axis runs over, the one named last changes fastest.
Arguments:
- tokens: bfloat16 [32768, 768], P(('rep', 'fsdp')), may hold values from -6 to 6
- bucket: int32 [32], P(('rep', 'fsdp')), may hold values from 0 to 1
- ln1_gain: bfloat16 [768], P('fsdp'), may hold values from 0.5 to 1.5
- ln1_bias: bfloat16 [768], P('fsdp'), may hold values from -3 to 3
- w_qkv: bfloat16 [768, 2304], P('fsdp'), may hold values from -0.21875 to 0.21875
- w_out: bfloat16 [768, 768], P('fsdp'), may hold values from -1.75 to 1.75
- ln2_gain: bfloat16 [768], P('fsdp'), may hold values from 0.5 to 1.5
- ln2_bias: bfloat16 [768], P('fsdp'), may hold values from -3 to 3
- w_up: bfloat16 [768, 3072], P('fsdp'), may hold values from -0.21875 to 0.21875
- w_down: bfloat16 [3072, 768], P('fsdp'), may hold values from -0.109375 to 0.109375
- cotangent: bfloat16 [32768, 768], P(('rep', 'fsdp')), may hold values from -6 to 6
Outputs:
- mixed: bfloat16 [32768, 768], P(('rep', 'fsdp'))
- tokens_grad: bfloat16 [32768, 768], P(('rep', 'fsdp'))
- ln1_gain_grad: float32 [768], P('fsdp')
- ln1_bias_grad: float32 [768], P('fsdp')
- w_qkv_grad: float32 [768, 2304], P('fsdp')
- w_out_grad: float32 [768, 768], P('fsdp')
- ln2_gain_grad: float32 [768], P('fsdp')
- ln2_bias_grad: float32 [768], P('fsdp')
- w_up_grad: float32 [768, 3072], P('fsdp')
- w_down_grad: float32 [3072, 768], P('fsdp')
Inputs may be any that keep to these rules, and one draw needn't show every extreme that they name: bucket is 1 where the device's 1024 tokens are one image and 0 where they are images of 256 tokens in a row.
All inputs are finite; a program needn't handle non-finite values.
Results may differ from a plain program's by a relative error of at most 0.019.
Values may be sent and summed in bfloat16 or wider, within the bound.
No kernel may reach another device: no remote copies, remote signals or barrier semaphores. Data moves between devices by JAX's collectives and lax.ppermute only.
A program may use at most 256 MiB of HBM per device.

v0:
```python
import jax
import jax.numpy as jnp
from jax import lax
from jax.sharding import PartitionSpec as P

HEAD_DIM = 64
SHORT = 256


norm_eps = 1e-06
masked_score = -1e30


def norm_rows(values, gain_vec, bias_vec):
    row_mean = jnp.mean(values, axis=-1, keepdims=True)
    centred = values - row_mean
    row_var = jnp.mean(centred * centred, axis=-1, keepdims=True)
    return centred * lax.rsqrt(row_var + norm_eps) * gain_vec + bias_vec


def gelu_exact(pre_act):
    return jax.nn.gelu(pre_act, approximate=False)


def dot_first(left, right):
    return lax.dot_general(
        left, right, (((0,), (0,)), ((), ())), preferred_element_type=jnp.float32
    )


def dot_last(left, right):
    return lax.dot_general(
        left, right, (((1,), (1,)), ((), ())), preferred_element_type=jnp.float32
    )


def shards(
    tokens, bucket, ln1_gain, ln1_bias, w_qkv, w_out, ln2_gain, ln2_bias, w_up, w_down, cotangent
):
    gathered = (
        lax.all_gather(ln1_gain, "fsdp", axis=0, tiled=True),
        lax.all_gather(ln1_bias, "fsdp", axis=0, tiled=True),
        lax.all_gather(w_qkv, "fsdp", axis=0, tiled=True),
        lax.all_gather(w_out, "fsdp", axis=0, tiled=True),
        lax.all_gather(ln2_gain, "fsdp", axis=0, tiled=True),
        lax.all_gather(ln2_bias, "fsdp", axis=0, tiled=True),
        lax.all_gather(w_up, "fsdp", axis=0, tiled=True),
        lax.all_gather(w_down, "fsdp", axis=0, tiled=True),
    )
    gain_one = gathered[0].astype(jnp.float32)
    bias_one = gathered[1].astype(jnp.float32)
    gain_two = gathered[4].astype(jnp.float32)
    bias_two = gathered[5].astype(jnp.float32)
    row_count = tokens.shape[0]
    width = tokens.shape[1]
    heads = width // HEAD_DIM
    scale = HEAD_DIM ** (-0.5)
    half_rows = row_count // 2
    positions = lax.iota(jnp.int32, row_count)
    segment = jnp.where(bucket[0] == 1, jnp.zeros_like(positions), positions // SHORT)
    inputs = tokens.astype(jnp.float32)
    normed_one = norm_rows(inputs, gain_one, bias_one).astype(jnp.bfloat16)
    qkv_low = jnp.dot(normed_one, gathered[2], preferred_element_type=jnp.float32).astype(
        jnp.bfloat16
    )
    queries = qkv_low[:, :width].reshape(row_count, heads, HEAD_DIM)
    keys_all = qkv_low[:, width : 2 * width].reshape(row_count, heads, HEAD_DIM)
    values_all = qkv_low[:, 2 * width :].reshape(row_count, heads, HEAD_DIM)
    query_blocks = queries.reshape(2, half_rows, heads, HEAD_DIM)
    segment_blocks = segment.reshape(2, half_rows)

    def block_scores(query_blk, segment_blk):
        scores = (
            jnp.einsum("qhd,khd->hqk", query_blk, keys_all, preferred_element_type=jnp.float32)
            * scale
        )
        allowed = segment_blk[:, None] == segment[None, :]
        return jnp.where(allowed[None], scores, masked_score)

    def forward_block(pair_item):
        query_blk, segment_blk = pair_item
        scores = block_scores(query_blk, segment_blk)
        top_score = jnp.max(scores, axis=-1, keepdims=True)
        expo = jnp.exp(scores - top_score)
        total = jnp.sum(expo, axis=-1, keepdims=True)
        probs_low = (expo / total).astype(jnp.bfloat16)
        att_blk = jnp.einsum(
            "hqk,khd->qhd", probs_low, values_all, preferred_element_type=jnp.float32
        )
        return (att_blk.astype(jnp.bfloat16), top_score + jnp.log(total))

    att_blocks, lse_blocks = lax.map(forward_block, (query_blocks, segment_blocks))
    attended = att_blocks.reshape(row_count, width)
    middle = inputs + jnp.dot(attended, gathered[3], preferred_element_type=jnp.float32)
    normed_two = norm_rows(middle, gain_two, bias_two).astype(jnp.bfloat16)
    up_value = jnp.dot(normed_two, gathered[6], preferred_element_type=jnp.float32)
    act_low = gelu_exact(up_value).astype(jnp.bfloat16)
    mixed = (middle + jnp.dot(act_low, gathered[7], preferred_element_type=jnp.float32)).astype(
        jnp.bfloat16
    )
    weights_back = (
        lax.all_gather(ln1_gain, "fsdp", axis=0, tiled=True),
        lax.all_gather(ln1_bias, "fsdp", axis=0, tiled=True),
        lax.all_gather(w_qkv, "fsdp", axis=0, tiled=True),
        lax.all_gather(w_out, "fsdp", axis=0, tiled=True),
        lax.all_gather(ln2_gain, "fsdp", axis=0, tiled=True),
        lax.all_gather(ln2_bias, "fsdp", axis=0, tiled=True),
        lax.all_gather(w_up, "fsdp", axis=0, tiled=True),
        lax.all_gather(w_down, "fsdp", axis=0, tiled=True),
    )
    grad_down_w = dot_first(act_low, cotangent)
    grad_act = dot_last(cotangent, weights_back[7])
    gelu_pull = jax.vjp(gelu_exact, up_value)[1]
    grad_up_value = gelu_pull(grad_act)[0].astype(jnp.bfloat16)
    grad_up_w = dot_first(normed_two, grad_up_value)
    grad_normed_two = dot_last(grad_up_value, weights_back[6])
    norm_two_pull = jax.vjp(norm_rows, middle, gain_two, bias_two)[1]
    grad_mid_norm, grad_gain_two, grad_bias_two = norm_two_pull(grad_normed_two)
    grad_middle = cotangent.astype(jnp.float32) + grad_mid_norm
    grad_branch = grad_middle.astype(jnp.bfloat16)
    grad_out_w = dot_first(attended, grad_branch)
    grad_attended = dot_last(grad_branch, weights_back[3]).astype(jnp.bfloat16)
    grad_att_blocks = grad_attended.reshape(2, half_rows, heads, HEAD_DIM)

    def backward_block(carry, pack_item):
        grad_keys, grad_values = carry
        query_blk, segment_blk, lse_blk, grad_att_blk = pack_item
        scores = block_scores(query_blk, segment_blk)
        probs = jnp.exp(scores - lse_blk)
        probs_low = probs.astype(jnp.bfloat16)
        grad_values = grad_values + jnp.einsum(
            "hqk,qhd->khd", probs_low, grad_att_blk, preferred_element_type=jnp.float32
        )
        grad_probs = jnp.einsum(
            "qhd,khd->hqk", grad_att_blk, values_all, preferred_element_type=jnp.float32
        )
        inner_sum = jnp.sum(probs * grad_probs, axis=-1, keepdims=True)
        grad_scores = (probs * (grad_probs - inner_sum)).astype(jnp.bfloat16)
        grad_query = (
            jnp.einsum("hqk,khd->qhd", grad_scores, keys_all, preferred_element_type=jnp.float32)
            * scale
        )
        grad_keys = (
            grad_keys
            + jnp.einsum("hqk,qhd->khd", grad_scores, query_blk, preferred_element_type=jnp.float32)
            * scale
        )
        return ((grad_keys, grad_values), grad_query)

    zero_heads = jnp.zeros((row_count, heads, HEAD_DIM), jnp.float32)
    (grad_keys, grad_values), grad_queries = lax.scan(
        backward_block,
        (zero_heads, zero_heads),
        (query_blocks, segment_blocks, lse_blocks, grad_att_blocks),
    )
    grad_qkv = jnp.concatenate(
        [
            grad_queries.reshape(row_count, width),
            grad_keys.reshape(row_count, width),
            grad_values.reshape(row_count, width),
        ],
        axis=1,
    ).astype(jnp.bfloat16)
    grad_qkv_w = dot_first(normed_one, grad_qkv)
    grad_normed_one = dot_last(grad_qkv, weights_back[2])
    norm_one_pull = jax.vjp(norm_rows, inputs, gain_one, bias_one)[1]
    grad_input_norm, grad_gain_one, grad_bias_one = norm_one_pull(grad_normed_one)
    tokens_grad = (grad_middle + grad_input_norm).astype(jnp.bfloat16)
    owned = (
        lax.psum_scatter(
            grad_gain_one.astype(jnp.bfloat16), "fsdp", scatter_dimension=0, tiled=True
        ).astype(jnp.float32),
        lax.psum_scatter(
            grad_bias_one.astype(jnp.bfloat16), "fsdp", scatter_dimension=0, tiled=True
        ).astype(jnp.float32),
        lax.psum_scatter(
            grad_qkv_w.astype(jnp.bfloat16), "fsdp", scatter_dimension=0, tiled=True
        ).astype(jnp.float32),
        lax.psum_scatter(
            grad_out_w.astype(jnp.bfloat16), "fsdp", scatter_dimension=0, tiled=True
        ).astype(jnp.float32),
        lax.psum_scatter(
            grad_gain_two.astype(jnp.bfloat16), "fsdp", scatter_dimension=0, tiled=True
        ).astype(jnp.float32),
        lax.psum_scatter(
            grad_bias_two.astype(jnp.bfloat16), "fsdp", scatter_dimension=0, tiled=True
        ).astype(jnp.float32),
        lax.psum_scatter(
            grad_up_w.astype(jnp.bfloat16), "fsdp", scatter_dimension=0, tiled=True
        ).astype(jnp.float32),
        lax.psum_scatter(
            grad_down_w.astype(jnp.bfloat16), "fsdp", scatter_dimension=0, tiled=True
        ).astype(jnp.float32),
    )
    final_grads = (
        lax.psum(owned[0].astype(jnp.bfloat16), "rep").astype(jnp.float32),
        lax.psum(owned[1].astype(jnp.bfloat16), "rep").astype(jnp.float32),
        lax.psum(owned[2].astype(jnp.bfloat16), "rep").astype(jnp.float32),
        lax.psum(owned[3].astype(jnp.bfloat16), "rep").astype(jnp.float32),
        lax.psum(owned[4].astype(jnp.bfloat16), "rep").astype(jnp.float32),
        lax.psum(owned[5].astype(jnp.bfloat16), "rep").astype(jnp.float32),
        lax.psum(owned[6].astype(jnp.bfloat16), "rep").astype(jnp.float32),
        lax.psum(owned[7].astype(jnp.bfloat16), "rep").astype(jnp.float32),
    )
    return (
        mixed,
        tokens_grad,
        final_grads[0],
        final_grads[1],
        final_grads[2],
        final_grads[3],
        final_grads[4],
        final_grads[5],
        final_grads[6],
        final_grads[7],
    )


def solution(mesh):
    return jax.shard_map(
        shards,
        mesh=mesh,
        in_specs=(
            P(("rep", "fsdp"), None),
            P(("rep", "fsdp")),
            P("fsdp"),
            P("fsdp"),
            P("fsdp", None),
            P("fsdp", None),
            P("fsdp"),
            P("fsdp"),
            P("fsdp", None),
            P("fsdp", None),
            P(("rep", "fsdp"), None),
        ),
        out_specs=(
            P(("rep", "fsdp"), None),
            P(("rep", "fsdp"), None),
            P("fsdp"),
            P("fsdp"),
            P("fsdp", None),
            P("fsdp", None),
            P("fsdp"),
            P("fsdp"),
            P("fsdp", None),
            P("fsdp", None),
        ),
        check_vma=False,
    )
```

profile of v0, /device:TPU:0, one launch (start us, length us, event | category | flops | bytes accessed | tf_op | source)
XLA Modules:
  0.0 692.4 jit_solution(15541294344394727113)
XLA Ops:
  16.1 15.7 %all-reduce.9 = (bf16[768]{0:T(1024)(128)(2,1)S(1)}, bf16[768]{0:T(1024)(128)(2,1)S(1)}, bf16[768]{0:T(1024)(128)(2,1)S(1)}, bf16[768]{0:T(1024)(128)(2,1)S(1)}) all-reduce(bf16[768]{0:T(1024)(128)(2,1)S(1)} %dynamic-update-slice.1, bf16[768]{0:T(1024)(128)(2,1)S(1)} %dynamic-update-slice, ...), channel_id=1, replica_groups=mesh['rep'=4,'fsdp'=8] {'fsdp'}, use_global_device_ids=true, to_apply=%add.1 | all-reduce | flops 3072 | bytes 12288
  37.5 9.3 %all-gather.5.cloned.1.call-done = bf16[768,2304]{1,0:T(8,128)(2,1)} async-done(((bf16[96,2304]{1,0:T(8,128)(2,1)}), bf16[768,2304]{1,0:T(8,128)(2,1)}) %all-gather.5.cloned.1.call-update) | async-done | bytes 3538960 | tf_op jit(solution)/shard_map/all_gather | solution.py:43
  46.8 6.4 convolution_convert_fusion
  59.6 3.9 reshape_reshape.3
  65.3 82.5 %while.28 = (s32[]{:T(128)}, bf16[2,512,12,64]{1,3,2,0:T(8,128)(2,1)}, f32[2,12,512,1]{2,1,3,0:T(8,128)S(1)}, s32[2,512]{1,0:T(2,128)S(1)}, bf16[2,512,12,64]{1,...) while((s32[]{:T(128)}, ...), condition=%wide.region_5.6_spmd.clone, body=%wide.region_2.5_spmd.clone.sunk | while | flops 1687030784 | bytes 189503664 | solution.py:92
  65.7 10.7 %fusion.126 = (f32[12,512]{1,0:T(8,128)S(1)}, f32[12,512,1024]{2,1,0:T(8,128)}) fusion(pred[512,1024]{1,0:T(8,128)(4,1)S(1)} %broadcast_compare_fusion.4, bf16[1024,12,64]{0,2,1:T(8,128)(2,1)S(1)} %get-tuple-element.487, bf16[2,512,12,64]{1,3,2,0:T(8,128)(2,1)S(1)} %get-tuple-element.486, s32[]{:T(128)S(6)} %copy.86), kind=kOutput, calls=%fused_computation.5.clone.1 | convolution fusion | flops 824174592 | bytes 28073988 | tf_op jit(solution)/shard_map/while/body/eval_jaxpr/qhd,khd->hqk/dot_general | solution.py:74
  76.3 12.7 %fusion.127 = f32[12,512]{1,0:T(8,128)S(1)} fusion(f32[12,512,1024]{2,1,0:T(8,128)} %get-tuple-element.449, f32[12,512]{1,0:T(8,128)S(1)} %get-tuple-element.450, pred[512,1024]{1,0:T(8,128)(4,1)S(1)} %broadcast_compare_fusion.4), kind=kLoop, calls=%fused_computation.6.clone.1 | loop fusion | flops 25159680 | bytes 25739264 | tf_op jit(solution)/shard_map/while/body/eval_jaxpr/reduce_sum | solution.py:85
  89.1 3.2 copy-done
  92.3 8.5 %fusion.128 = bf16[2,512,12,64]{1,3,2,0:T(8,128)(2,1)} fusion(bf16[2,512,12,64]{1,3,2,0:T(8,128)(2,1)} %get-tuple-element.474, s32[]{:T(128)S(6)} %copy.86, bf16[1024,12,64]{0,2,1:T(8,128)(2,1)S(1)} %copy-done.4, f32[12,512,1024]{2,1,0:T(8,128)S(1)} %copy-done, f32[12,512]{1,0:T(8,128)S(1)} %fusion.127, f32[12,512]{1,0:T(8,128)S(1)} %get-tuple-element.450, ...), kind=kOutput, calls=%fused_computation.10.clone.1 | convolution fusion | flops 837156864 | bytes 28098564 | tf_op jit(solution)/shard_map/while/body/eval_jaxpr/hqk,khd->qhd/dot_general | solution.py:87
  101.3 10.8 %fusion.126 = (f32[12,512]{1,0:T(8,128)S(1)}, f32[12,512,1024]{2,1,0:T(8,128)}) fusion(pred[512,1024]{1,0:T(8,128)(4,1)S(1)} %broadcast_compare_fusion.4, bf16[1024,12,64]{0,2,1:T(8,128)(2,1)S(1)} %get-tuple-element.487, bf16[2,512,12,64]{1,3,2,0:T(8,128)(2,1)S(1)} %get-tuple-element.486, s32[]{:T(128)S(6)} %copy.86), kind=kOutput, calls=%fused_computation.5.clone.1 | convolution fusion | flops 824174592 | bytes 28073988 | tf_op jit(solution)/shard_map/while/body/eval_jaxpr/qhd,khd->hqk/dot_general | solution.py:74
  112.1 12.7 %fusion.127 = f32[12,512]{1,0:T(8,128)S(1)} fusion(f32[12,512,1024]{2,1,0:T(8,128)} %get-tuple-element.449, f32[12,512]{1,0:T(8,128)S(1)} %get-tuple-element.450, pred[512,1024]{1,0:T(8,128)(4,1)S(1)} %broadcast_compare_fusion.4), kind=kLoop, calls=%fused_computation.6.clone.1 | loop fusion | flops 25159680 | bytes 25739264 | tf_op jit(solution)/shard_map/while/body/eval_jaxpr/reduce_sum | solution.py:85
  124.8 3.4 copy-done
  128.2 8.5 %fusion.128 = bf16[2,512,12,64]{1,3,2,0:T(8,128)(2,1)} fusion(bf16[2,512,12,64]{1,3,2,0:T(8,128)(2,1)} %get-tuple-element.474, s32[]{:T(128)S(6)} %copy.86, bf16[1024,12,64]{0,2,1:T(8,128)(2,1)S(1)} %copy-done.4, f32[12,512,1024]{2,1,0:T(8,128)S(1)} %copy-done, f32[12,512]{1,0:T(8,128)S(1)} %fusion.127, f32[12,512]{1,0:T(8,128)S(1)} %get-tuple-element.450, ...), kind=kOutput, calls=%fused_computation.10.clone.1 | convolution fusion | flops 837156864 | bytes 28098564 | tf_op jit(solution)/shard_map/while/body/eval_jaxpr/hqk,khd->qhd/dot_general | solution.py:87
  147.7 3.0 copy.60
  152.3 3.9 fusion.78
  158.4 37.3 %multiply_convert_fusion.1 = (bf16[1024,3072]{1,0:T(8,128)(2,1)}, f32[1024,3072]{1,0:T(8,128)}, f32[1024,3072]{1,0:T(8,128)}) fusion(bf16[768,3072]{1,0:T(8,128)(2,1)} %all-gather.9.cloned.1.call-done, f32[1024,768]{0,1:T(8,128)} %copy-done.8, f32[768]{0:T(1024)S(1)} %copy-done.41, f32[768]{0:T(1024)S(1)} %copy-done.34, f32[1024]{0:T(1024)S(1)} %fusion.68, ...), kind=kOutput, calls=%fused_computation.67 | convolution fusion | flops 5040242688 | bytes 39335936 | tf_op jit(solution)/shard_map/dot_general | solution.py:96
  195.7 17.5 %add_convert_fusion = bf16[1024,3072]{1,0:T(8,128)(2,1)} fusion(f32[1024,3072]{1,0:T(8,128)} %get-tuple-element.323, f32[1024,3072]{1,0:T(8,128)} %get-tuple-element.335, bf16[1024,768]{1,0:T(8,128)(2,1)} %param.25, bf16[3072,768]{1,0:T(8,128)(2,1)} %all-gather.11.cloned.1.call-done), kind=kOutput, calls=%fused_computation.66 | convolution fusion | flops 4875878400 | bytes 37748736 | tf_op jit(solution)/shard_map/dot_general | solution.py:32
  213.2 9.5 %fusion.80 = (bf16[768]{0:T(1024)(128)(2,1)}, f32[1024,768]{1,0:T(8,128)}) fusion(bf16[1024,3072]{1,0:T(8,128)(2,1)} %add_convert_fusion, bf16[768,3072]{1,0:T(8,128)(2,1)S(1)} %copy-done.46), kind=kOutput, calls=%fused_computation.137 | convolution fusion | flops 4832623616 | bytes 14157312 | tf_op jit(solution)/shard_map/dot_general | solution.py:32
  222.7 3.5 copy.63
  226.3 4.5 multiply_reduce_fusion.1
  237.0 4.3 convolution_convert_fusion.4
  243.9 3.8 reshape.205
  250.7 170.7 %while.29 = (s32[]{:T(128)}, f32[1024,12,64]{0,2,1:T(8,128)}, f32[1024,12,64]{0,2,1:T(8,128)}, bf16[2,512,12,64]{1,3,2,0:T(8,128)(2,1)}, bf16[2,512,12,64]{1,3,2...) while((s32[]{:T(128)}, f32[1024,12,64]{0,2,1:T(8,128)}, ...), condition=%wide.region_12.13_spmd.clone, body=%wide.region_10.12_spmd.clone.sunk | while | flops 4125756416 | bytes 231930096 | solution.py:151
  252.4 11.8 %fusion.138 = f32[12,512,1024]{2,1,0:T(8,128)} fusion(bf16[1024,12,64]{0,2,1:T(8,128)(2,1)S(1)} %get-tuple-element.523, bf16[2,512,12,64]{1,3,2,0:T(8,128)(2,1)} %copy-done.2, s32[]{:T(128)S(6)} %copy.96), kind=kOutput, calls=%fused_computation.42.clone.1 | convolution fusion | flops 805306368 | bytes 27525124 | tf_op jit(solution)/shard_map/while/body/eval_jaxpr/qhd,khd->hqk/dot_general | solution.py:74
  264.3 13.6 %bitcast_add_fusion.5 = f32[1024,12,64]{0,2,1:T(8,128)} fusion(f32[1024,12,64]{0,2,1:T(8,128)} %get-tuple-element.506, f32[12,512,1024]{2,1,0:T(8,128)} %fusion.138, f32[12,512]{1,0:T(8,128)S(1)} %dynamic-slice_bitcast_fusion.2, pred[512,1024]{1,0:T(8,128)(4,1)S(1)} %broadcast_compare_fusion.5, pred[]{:T(512)S(6)} %compare.7, ...), kind=kOutput, calls=%fused_computation.34.clone.1 | convolution fusion | flops 832045056 | bytes 32800772 | tf_op jit(solution)/shard_map/while/body/eval_jaxpr/hqk,qhd->khd/dot_general | solution.py:131
  277.9 18.1 %multiply_reduce_fusion.5 = (f32[12,512]{1,0:T(8,128)S(1)}, f32[12,512,1024]{2,1,0:T(8,128)}) fusion(f32[12,512,1024]{2,1,0:T(8,128)} %fusion.138, f32[12,512]{1,0:T(8,128)S(1)} %dynamic-slice_bitcast_fusion.2, pred[512,1024]{1,0:T(8,128)(4,1)S(1)} %broadcast_compare_fusion.5, bf16[1024,12,64]{0,2,1:T(8,128)(2,1)} %get-tuple-element.526, ...), kind=kOutput, calls=%fused_computation.29.clone.1 | convolution fusion | flops 836757504 | bytes 53264388 | tf_op jit(solution)/shard_map/while/body/eval_jaxpr/qhd,khd->hqk/dot_general | solution.py:134
  296.0 21.2 %multiply_convert_fusion.3 = bf16[12,512,1024]{2,1,0:T(8,128)(2,1)} fusion(f32[12,512,1024]{2,1,0:T(8,128)} %get-tuple-element.462, f32[12,512,1024]{2,1,0:T(8,128)} %fusion.138, f32[12,512]{1,0:T(8,128)S(1)} %get-tuple-element.463, f32[12,512]{1,0:T(8,128)S(1)} %dynamic-slice_bitcast_fusion.2, pred[512,1024]{1,0:T(8,128)(4,1)S(1)} %broadcast_compare_fusion.5), kind=kLoop, calls=%fused_computation.28.clone.1 | loop fusion | flops 37748736 | bytes 63488000 | tf_op jit(solution)/shard_map/while/body/eval_jaxpr/convert_element_type | solution.py:138
  317.3 9.5 %bitcast_dynamic-update-slice_fusion.5 = bf16[2,512,12,64]{1,3,2,0:T(8,128)(2,1)} fusion(bf16[2,512,12,64]{1,3,2,0:T(8,128)(2,1)} %get-tuple-element.507, s32[]{:T(128)S(6)} %copy.96, bf16[12,512,1024]{2,1,0:T(8,128)(2,1)} %multiply_convert_fusion.3, bf16[1024,12,64]{0,2,1:T(8,128)(2,1)S(1)} %get-tuple-element.523), kind=kOutput, calls=%fused_computation.36.clone.1 | convolution fusion | flops 805699584 | bytes 15728644 | tf_op jit(solution)/shard_map/while/body/eval_jaxpr/hqk,khd->qhd/dot_general | solution.py:140
  326.8 8.6 %bitcast_add_fusion.4 = f32[1024,12,64]{0,2,1:T(8,128)} fusion(f32[1024,12,64]{0,2,1:T(8,128)} %get-tuple-element.505, bf16[12,512,1024]{2,1,0:T(8,128)(2,1)} %multiply_convert_fusion.3, pred[]{:T(512)S(6)} %compare.7, bf16[2,512,12,64]{1,3,2,0:T(8,128)(2,1)S(1)} %copy-done.3, s32[]{:T(128)S(6)} %copy.96), kind=kOutput, calls=%fused_computation.35.clone.1 | convolution fusion | flops 807665664 | bytes 19660804 | tf_op jit(solution)/shard_map/while/body/eval_jaxpr/hqk,qhd->khd/dot_general | solution.py:145
  336.9 11.5 %fusion.138 = f32[12,512,1024]{2,1,0:T(8,128)} fusion(bf16[1024,12,64]{0,2,1:T(8,128)(2,1)S(1)} %get-tuple-element.523, bf16[2,512,12,64]{1,3,2,0:T(8,128)(2,1)} %copy-done.2, s32[]{:T(128)S(6)} %copy.96), kind=kOutput, calls=%fused_computation.42.clone.1 | convolution fusion | flops 805306368 | bytes 27525124 | tf_op jit(solution)/shard_map/while/body/eval_jaxpr/qhd,khd->hqk/dot_general | solution.py:74
  348.4 14.3 %bitcast_add_fusion.5 = f32[1024,12,64]{0,2,1:T(8,128)} fusion(f32[1024,12,64]{0,2,1:T(8,128)} %get-tuple-element.506, f32[12,512,1024]{2,1,0:T(8,128)} %fusion.138, f32[12,512]{1,0:T(8,128)S(1)} %dynamic-slice_bitcast_fusion.2, pred[512,1024]{1,0:T(8,128)(4,1)S(1)} %broadcast_compare_fusion.5, pred[]{:T(512)S(6)} %compare.7, ...), kind=kOutput, calls=%fused_computation.34.clone.1 | convolution fusion | flops 832045056 | bytes 32800772 | tf_op jit(solution)/shard_map/while/body/eval_jaxpr/hqk,qhd->khd/dot_general | solution.py:131
  362.7 18.1 %multiply_reduce_fusion.5 = (f32[12,512]{1,0:T(8,128)S(1)}, f32[12,512,1024]{2,1,0:T(8,128)}) fusion(f32[12,512,1024]{2,1,0:T(8,128)} %fusion.138, f32[12,512]{1,0:T(8,128)S(1)} %dynamic-slice_bitcast_fusion.2, pred[512,1024]{1,0:T(8,128)(4,1)S(1)} %broadcast_compare_fusion.5, bf16[1024,12,64]{0,2,1:T(8,128)(2,1)} %get-tuple-element.526, ...), kind=kOutput, calls=%fused_computation.29.clone.1 | convolution fusion | flops 836757504 | bytes 53264388 | tf_op jit(solution)/shard_map/while/body/eval_jaxpr/qhd,khd->hqk/dot_general | solution.py:134
  380.8 21.2 %multiply_convert_fusion.3 = bf16[12,512,1024]{2,1,0:T(8,128)(2,1)} fusion(f32[12,512,1024]{2,1,0:T(8,128)} %get-tuple-element.462, f32[12,512,1024]{2,1,0:T(8,128)} %fusion.138, f32[12,512]{1,0:T(8,128)S(1)} %get-tuple-element.463, f32[12,512]{1,0:T(8,128)S(1)} %dynamic-slice_bitcast_fusion.2, pred[512,1024]{1,0:T(8,128)(4,1)S(1)} %broadcast_compare_fusion.5), kind=kLoop, calls=%fused_computation.28.clone.1 | loop fusion | flops 37748736 | bytes 63488000 | tf_op jit(solution)/shard_map/while/body/eval_jaxpr/convert_element_type | solution.py:138
  402.1 9.5 %bitcast_dynamic-update-slice_fusion.5 = bf16[2,512,12,64]{1,3,2,0:T(8,128)(2,1)} fusion(bf16[2,512,12,64]{1,3,2,0:T(8,128)(2,1)} %get-tuple-element.507, s32[]{:T(128)S(6)} %copy.96, bf16[12,512,1024]{2,1,0:T(8,128)(2,1)} %multiply_convert_fusion.3, bf16[1024,12,64]{0,2,1:T(8,128)(2,1)S(1)} %get-tuple-element.523), kind=kOutput, calls=%fused_computation.36.clone.1 | convolution fusion | flops 805699584 | bytes 15728644 | tf_op jit(solution)/shard_map/while/body/eval_jaxpr/hqk,khd->qhd/dot_general | solution.py:140
  411.6 9.5 %bitcast_add_fusion.4 = f32[1024,12,64]{0,2,1:T(8,128)} fusion(f32[1024,12,64]{0,2,1:T(8,128)} %get-tuple-element.505, bf16[12,512,1024]{2,1,0:T(8,128)(2,1)} %multiply_convert_fusion.3, pred[]{:T(512)S(6)} %compare.7, bf16[2,512,12,64]{1,3,2,0:T(8,128)(2,1)S(1)} %copy-done.3, s32[]{:T(128)S(6)} %copy.96), kind=kOutput, calls=%fused_computation.35.clone.1 | convolution fusion | flops 807665664 | bytes 19660804 | tf_op jit(solution)/shard_map/while/body/eval_jaxpr/hqk,qhd->khd/dot_general | solution.py:145
  421.5 3.2 copy.67
  429.7 5.9 convolution_convert_fusion.3
  436.3 10.0 %convolution_convert_fusion.2 = bf16[768,3072]{1,0:T(8,128)(2,1)} fusion(bf16[1024,3072]{1,0:T(8,128)(2,1)} %add_convert_fusion, f32[1024,768]{0,1:T(8,128)} %copy-done.8, f32[768]{0:T(1024)S(1)} %copy-done.42, f32[768]{0:T(1024)S(1)} %copy-done.35, f32[1024]{0:T(1024)S(1)} %copy-done.39, f32[1024]{0:T(1024)S(1)} %copy-done.29), kind=kOutput, calls=%fused_computation.83 | convolution fusion | flops 4838129664 | bytes 14170112 | tf_op jit(solution)/shard_map/dot_general | solution.py:26
  447.8 10.0 %convolution_convert_fusion.1 = bf16[3072,768]{1,0:T(8,128)(2,1)} fusion(bf16[1024,3072]{1,0:T(8,128)(2,1)} %get-tuple-element.322, bf16[1024,768]{1,0:T(8,128)(2,1)S(1)} %copy-done.16), kind=kOutput, calls=%fused_computation.82 | convolution fusion | flops 4834197504 | bytes 12582912 | tf_op jit(solution)/shard_map/dot_general | solution.py:26
  458.5 10.1 %add_convert_fusion.2 = bf16[1024,768]{0,1:T(8,128)(2,1)} fusion(f32[1024,768]{0,1:T(8,128)} %copy-done.8, bf16[1024,3072]{1,0:T(8,128)(2,1)} %get-tuple-element.322, bf16[3072,768]{1,0:T(8,128)(2,1)} %all-gather.11.cloned.1.call-done), kind=kOutput, calls=%fused_computation.106 | convolution fusion | flops 4833411072 | bytes 15728640 | tf_op jit(solution)/shard_map/dot_general | solution.py:98
  471.3 8.6 %fusion.79 = (bf16[768]{0:T(1024)(128)(2,1)S(1)}, f32[1024,768]{1,0:T(8,128)}) fusion(bf16[768,2304]{1,0:T(8,128)(2,1)} %all-gather.5.cloned.1.call-done, bf16[1024,768]{0,1:T(8,128)(2,1)} %bitcast.134, bf16[1024,768]{0,1:T(8,128)(2,1)} %bitcast.132, bf16[1024,768]{0,1:T(8,128)(2,1)S(1)} %bitcast.128), kind=kOutput, calls=%fused_computation.136 | convolution fusion | flops 3638820096 | bytes 11404800 | tf_op jit(solution)/shard_map/dot_general | solution.py:32
  479.9 3.6 copy.68
  483.9 57.8 %reduce-scatter.9.cloned.1.call-done = bf16[96,3072]{1,0:T(8,128)(2,1)} async-done(((bf16[768,3072]{1,0:T(8,128)(2,1)}), bf16[96,3072]{1,0:T(8,128)(2,1)}) %reduce-scatter.9.cloned.1.call-update) | async-done | bytes 589840 | tf_op jit(solution)/shard_map/reduce_scatter | solution.py:188
  541.6 57.3 %reduce-scatter.11.cloned.1.call-done = bf16[384,768]{1,0:T(8,128)(2,1)} async-done(((bf16[3072,768]{1,0:T(8,128)(2,1)}), bf16[384,768]{1,0:T(8,128)(2,1)}) %reduce-scatter.11.cloned.1.call-update) | async-done | bytes 589840 | tf_op jit(solution)/shard_map/reduce_scatter | solution.py:191
  603.2 13.4 %all-reduce.8 = (bf16[768]{0:T(1024)(128)(2,1)S(1)}, bf16[768]{0:T(1024)(128)(2,1)S(1)}, bf16[768]{0:T(1024)(128)(2,1)S(1)}, bf16[768]{0:T(1024)(128)(2,1)S(1)}) all-reduce(bf16[768]{0:T(1024)(128)(2,1)S(1)} %get-tuple-element.264, bf16[768]{0:T(1024)(128)(2,1)S(1)} %get-tuple-element.336, ...), channel_id=2, replica_groups=mesh['rep'=4,'fsdp'=8] {'fsdp'}, use_global_device_ids=true, to_apply=%region_16.17.clone | all-reduce | flops 3072 | bytes 12288
  616.8 12.4 %all-reduce.10 = (bf16[96]{0:T(256)(128)(2,1)S(1)}, bf16[96]{0:T(256)(128)(2,1)S(1)}, bf16[96]{0:T(256)(128)(2,1)S(1)}, bf16[96]{0:T(256)(128)(2,1)S(1)}) all-reduce(bf16[96]{0:T(256)(128)(2,1)S(1)} %dynamic-slice.5, bf16[96]{0:T(256)(128)(2,1)S(1)} %dynamic-slice.7, ...), channel_id=1, replica_groups=mesh['rep'=4,'fsdp'=8] {'rep'}, use_global_device_ids=true, to_apply=%region_17.18 | all-reduce | flops 384 | bytes 1536 | tf_op jit(solution)/shard_map/psum | solution.py:196
  631.3 5.5 add_convert_fusion.1
  639.4 39.3 %all-reduce.14.cloned.1.call-done = (bf16[96,2304]{1,0:T(8,128)(2,1)}, bf16[96,768]{1,0:T(8,128)(2,1)}, bf16[96,3072]{1,0:T(8,128)(2,1)}, bf16[384,768]{1,0:T(8,128)(2,1)}) async-done(((bf16[96,2304]{1,0:T(8,128)(2,1)}, bf16[96,768]{1,0:T(8,128)(2,1)}, bf16[96,3072]{1,0:T(8,128)(2,1)}, bf16[384,768]{1,0:T(8,128)(2,1)}), (bf16[96,2304]{1,0:T(8,128)(2,1)}, bf16[96,768]{1,0:T(8,128)(2,1)}, ...) | async-done | bytes 1769488 | tf_op jit(solution)/shard_map/psum | solution.py:198
  (203 shorter events, 66.7 us)
Async XLA Ops:
  7.2 39.6 %all-gather.5.cloned.1.call-start = ((), (), s32[]{:S(2)}) async-start(), calls=%async_computation.4 | async-start | bytes 3981312 | tf_op jit(solution)/shard_map/all_gather | solution.py:43
  7.9 144.4 %all-gather.7.cloned.1.call-start = ((), (), s32[]{:S(2)}) async-start(), calls=%async_computation.5 | async-start | bytes 1327104 | tf_op jit(solution)/shard_map/all_gather | solution.py:44
  8.7 149.7 %all-gather.9.cloned.1.call-start = ((), (), s32[]{:S(2)}) async-start(), calls=%async_computation.6 | async-start | bytes 5308416 | tf_op jit(solution)/shard_map/all_gather | solution.py:47
  9.4 186.3 %all-gather.11.cloned.1.call-start = ((), (), s32[]{:S(2)}) async-start(), calls=%async_computation.7 | async-start | bytes 5308416 | tf_op jit(solution)/shard_map/all_gather | solution.py:48
  10.0 473.6 %reduce-scatter.7.cloned.1.call-start = ((), (), s32[]{:S(2)}) async-start(), calls=%async_computation.9 | async-start | bytes 1327104 | tf_op jit(solution)/shard_map/reduce_scatter | solution.py:179
  31.8 15.0 %copy-start.43 = (f32[768]{0:T(1024)}, f32[768]{0:T(1024)S(1)}, u32[]{:S(2)}) copy-start(f32[768]{0:T(1024)S(1)} %convert_element_type.127) | copy-start | bytes 9220
  31.8 15.0 %copy-start.26 = (f32[768]{0:T(1024)}, f32[768]{0:T(1024)S(1)}, u32[]{:S(2)}) copy-start(f32[768]{0:T(1024)S(1)} %convert_element_type.126) | copy-start | bytes 9220
  33.0 2.9 copy-start.15
  35.1 11.7 %copy-start.5 = (bf16[1024,768]{0,1:T(8,128)(2,1)}, bf16[1024,768]{0,1:T(8,128)(2,1)S(1)}, u32[]{:S(2)}) copy-start(bf16[1024,768]{0,1:T(8,128)(2,1)S(1)} %copy.55) | copy-start | bytes 4718596
  35.4 17.8 %copy-start.24 = (f32[1024]{0:T(1024)}, f32[1024]{0:T(1024)S(1)}, u32[]{:S(2)}) copy-start(f32[1024]{0:T(1024)S(1)} %broadcast_multiply_fusion.1) | copy-start | bytes 12292
  35.9 17.4 %copy-start.32 = (f32[1024]{0:T(1024)}, f32[1024]{0:T(1024)S(1)}, u32[]{:S(2)}) copy-start(f32[1024]{0:T(1024)S(1)} %fusion.61) | copy-start | bytes 12292
  35.9 17.3 %copy-start.30 = (f32[1024]{0:T(1024)}, f32[1024]{0:T(1024)S(1)}, u32[]{:S(2)}) copy-start(f32[1024]{0:T(1024)S(1)} %fusion.67) | copy-start | bytes 12292
  65.7 23.4 %copy-start.4 = (bf16[1024,12,64]{0,2,1:T(8,128)(2,1)S(1)}, bf16[1024,12,64]{0,2,1:T(8,128)(2,1)}, u32[]{:S(2)}) copy-start(bf16[1024,12,64]{0,2,1:T(8,128)(2,1)} %get-tuple-element.488) | copy-start | bytes 4718596 | tf_op jit(solution)/shard_map/while
  76.3 16.0 %copy-start = (f32[12,512,1024]{2,1,0:T(8,128)S(1)}, f32[12,512,1024]{2,1,0:T(8,128)}, u32[]{:S(2)}) copy-start(f32[12,512,1024]{2,1,0:T(8,128)} %get-tuple-element.449) | copy-start | bytes 75497472 | tf_op jit(solution)/shard_map/while
  101.3 23.5 %copy-start.4 = (bf16[1024,12,64]{0,2,1:T(8,128)(2,1)S(1)}, bf16[1024,12,64]{0,2,1:T(8,128)(2,1)}, u32[]{:S(2)}) copy-start(bf16[1024,12,64]{0,2,1:T(8,128)(2,1)} %get-tuple-element.488) | copy-start | bytes 4718596 | tf_op jit(solution)/shard_map/while
  112.1 16.1 %copy-start = (f32[12,512,1024]{2,1,0:T(8,128)S(1)}, f32[12,512,1024]{2,1,0:T(8,128)}, u32[]{:S(2)}) copy-start(f32[12,512,1024]{2,1,0:T(8,128)} %get-tuple-element.449) | copy-start | bytes 75497472 | tf_op jit(solution)/shard_map/while
  156.2 1.7 copy-start.8
  156.2 2.1 copy-start.34
  156.2 2.1 copy-start.41
  156.2 74.5 %copy-start.28 = (f32[1024]{0:T(1024)}, f32[1024]{0:T(1024)S(1)}, u32[]{:S(2)}) copy-start(f32[1024]{0:T(1024)S(1)} %broadcast_multiply_fusion) | copy-start | bytes 12292
  158.3 72.5 %copy-start.38 = (f32[1024]{0:T(1024)}, f32[1024]{0:T(1024)S(1)}, u32[]{:S(2)}) copy-start(f32[1024]{0:T(1024)S(1)} %fusion.68) | copy-start | bytes 12292
  195.7 17.5 %copy-start.46 = (bf16[768,3072]{1,0:T(8,128)(2,1)S(1)}, bf16[768,3072]{1,0:T(8,128)(2,1)}, u32[]{:S(2)}) copy-start(bf16[768,3072]{1,0:T(8,128)(2,1)} %all-gather.9.cloned.1.call-done) | copy-start | bytes 14155780
  226.2 4.5 copy-start.9
  226.3 4.7 copy-start.10
  231.7 1.7 copy-start.11
  232.4 2.2 copy-start.19
  250.7 233.2 %reduce-scatter.5.cloned.1.call-start = ((), (), s32[]{:S(2)}) async-start(), calls=%async_computation.8 | async-start | bytes 3981312 | tf_op jit(solution)/shard_map/reduce_scatter | solution.py:176
  252.4 11.9 %copy-start.12 = (bf16[2,512,12,64]{1,3,2,0:T(8,128)(2,1)S(1)}, bf16[2,512,12,64]{1,3,2,0:T(8,128)(2,1)}, u32[]{:S(2)}) copy-start(bf16[2,512,12,64]{1,3,2,0:T(8,128)(2,1)} %get-tuple-element.525) | copy-start | bytes 4718596 | tf_op jit(solution)/shard_map/while
  317.3 9.5 %copy-start.3 = (bf16[2,512,12,64]{1,3,2,0:T(8,128)(2,1)S(1)}, bf16[2,512,12,64]{1,3,2,0:T(8,128)(2,1)}, u32[]{:S(2)}) copy-start(bf16[2,512,12,64]{1,3,2,0:T(8,128)(2,1)} %copy-done.2) | copy-start | bytes 4718596 | tf_op jit(solution)/shard_map/while
  336.9 11.5 %copy-start.12 = (bf16[2,512,12,64]{1,3,2,0:T(8,128)(2,1)S(1)}, bf16[2,512,12,64]{1,3,2,0:T(8,128)(2,1)}, u32[]{:S(2)}) copy-start(bf16[2,512,12,64]{1,3,2,0:T(8,128)(2,1)} %get-tuple-element.525) | copy-start | bytes 4718596 | tf_op jit(solution)/shard_map/while
  402.1 9.5 %copy-start.3 = (bf16[2,512,12,64]{1,3,2,0:T(8,128)(2,1)S(1)}, bf16[2,512,12,64]{1,3,2,0:T(8,128)(2,1)}, u32[]{:S(2)}) copy-start(bf16[2,512,12,64]{1,3,2,0:T(8,128)(2,1)} %copy-done.2) | copy-start | bytes 4718596 | tf_op jit(solution)/shard_map/while
  421.4 3.6 copy-start.1
  425.1 3.4 copy-start.17
  425.3 3.1 copy-start.20
  425.3 4.3 copy-start.6
  425.3 4.3 copy-start.25
  425.4 4.3 copy-start.27
  425.4 4.3 copy-start.31
  425.4 4.3 copy-start.44
  435.6 106.0 %reduce-scatter.9.cloned.1.call-start = ((), (), s32[]{:S(2)}) async-start(), calls=%async_computation.10 | async-start | bytes 5308416 | tf_op jit(solution)/shard_map/reduce_scatter | solution.py:188
  446.3 152.7 %reduce-scatter.11.cloned.1.call-start = ((), (), s32[]{:S(2)}) async-start(), calls=%async_computation.11 | async-start | bytes 5308416 | tf_op jit(solution)/shard_map/reduce_scatter | solution.py:191
  457.8 220.9 %all-reduce.14.cloned.1.call-start = ((), (), s32[]{:S(2)}) async-start(), calls=%async_computation.12 | async-start | bytes 3538944 | tf_op jit(solution)/shard_map/psum | solution.py:198
  468.6 2.7 copy-start.18
  598.9 2.6 copy-start.33
  599.0 2.8 copy-start.7
  601.6 29.7 %copy-start.14 = (bf16[1024,768]{0,1:T(8,128)(2,1)S(1)}, bf16[1024,768]{0,1:T(8,128)(2,1)}, u32[]{:S(2)}) copy-start(bf16[1024,768]{0,1:T(8,128)(2,1)} %copy.62) | copy-start | bytes 4718596
  601.6 29.7 %copy-start.37 = (f32[1024]{0:T(1024)S(1)}, f32[1024]{0:T(1024)}, u32[]{:S(2)}) copy-start(f32[1024]{0:T(1024)} %copy-done.36) | copy-start | bytes 12292
  678.7 5.9 copy-start.23
  (13 other events, 15.2 us)
Sparse Core Ops, SparseCore 0:
  9.9 36.8 all-gather.4
  48.7 24.0 all-gather.6
  74.6 38.9 all-gather.8
  115.3 38.9 all-gather.10
  250.8 36.7 reduce-scatter.6
  435.7 48.0 reduce-scatter.4
  487.7 53.8 reduce-scatter.8
  545.1 53.8 reduce-scatter.10
  601.8 76.8 all-reduce.13
where the time goes:
time: 702 us; the launch traced here: 692 us
  matrix products  289 us (41%)
  waiting for transfers between devices  167 us (24%)
  other arithmetic  99.3 us (14%)
  local copies, waits for them, and re-layouts  67.1 us (10%)
  blocking collectives  41.4 us (6%)
  between operations  16.6 us (2%)
  loops' own time  11.8 us (2%)
    reduce_scatter x1, waiting for transfers between devices, shards(): lax.psum_scatter(grad_up_w.astype(jnp.bfloat16), 'fsdp', scatter_dimensio...  57.8 us
    reduce_scatter x1, waiting for transfers between devices, shards(): lax.psum_scatter(grad_down_w.astype(jnp.bfloat16), 'fsdp', scatter_dimens...  57.3 us
    dot_general x4, matrix products, block_scores(): jnp.einsum('qhd,khd->hqk', query_blk, keys_all, preferred_element_type=jn...  44.8 us
    convert_element_type x2, other arithmetic, backward_block(): grad_scores = (probs * (grad_probs - inner_sum)).astype(jnp.bfloat16)  42.5 us
    dot_general x4, matrix products, dot_last(): lax.dot_general(left, right, (((1,), (1,)), ((), ())), preferred_element_...  40 us
    psum x1, waiting for transfers between devices, shards(): lax.psum(owned[2].astype(jnp.bfloat16), 'rep').astype(jnp.float32)  39.3 us
    dot_general x1, matrix products, shards(): jnp.dot(normed_two, gathered[6], preferred_element_type=jnp.float32)  37.3 us
    dot_general x2, matrix products, backward_block(): jnp.einsum('qhd,khd->hqk', grad_att_blk, values_all, preferred_element_ty...  36.3 us
  transfers between devices with their start and end apart: 9, of which 5 were waited for; matrix products, arithmetic and copies ran while one was open for 55% of the time, Pallas kernels for 0%

commit v1 on v0

v1 whole, which is shorter than its diff:
```python
import functools

import jax
import jax.numpy as jnp
from jax import lax
from jax.experimental import pallas as pl
from jax.experimental.pallas import tpu as pltpu
from jax.sharding import PartitionSpec as P

HD=64; SHORT=256; LN_EPS=1e-6
f32=jnp.float32; bf16=jnp.bfloat16
def nt(a,b): return lax.dot_general(a,b,(((1,),(1,)),((),())),preferred_element_type=f32)
def nn(a,b): return lax.dot_general(a,b,(((1,),(0,)),((),())),preferred_element_type=f32)
def tn(a,b): return lax.dot_general(a,b,(((0,),(0,)),((),())),preferred_element_type=f32)

def ln_rows(x,g,b):
    mu=jnp.mean(x,axis=-1,keepdims=True); c=x-mu
    var=jnp.mean(c*c,axis=-1,keepdims=True)
    return c*lax.rsqrt(var+LN_EPS)*g+b

def terms(v):
    hi=v.astype(bf16).astype(f32); r=v-hi
    mid=r.astype(bf16).astype(f32)
    return hi,mid,r-mid

def ext(own,val,lane,base,v3):
    h,m,l=v3
    return jnp.where(own,val,jnp.where(lane==base,h,jnp.where(lane==base+1,m,jnp.where(lane==base+2,l,0.0)))).astype(bf16)

def fwd_kernel(QB,bucket_ref,x_ref,g_ref,b_ref,wq_ref,wk_ref,wv_ref,n1_ref,qe_ref,k_ref,v_ref,att_ref,vx_ref):
    T=x_ref.shape[0]; RB=128
    @pl.when(pl.program_id(0)==0)
    def _():
        def body(i,_):
            r=pl.ds(i*RB,RB)
            n1_ref[r,:]=ln_rows(x_ref[r,:].astype(f32),g_ref[...],b_ref[...]).astype(bf16)
            return 0
        lax.fori_loop(0,T//RB,body,0)
    n1=n1_ref[...]
    lane=lax.broadcasted_iota(jnp.int32,(T,128),1)
    low=lane<64
    q=nn(n1,wq_ref[...])
    for p in range(2):
        qp=q[:,128*p:128*p+128]*0.125
        qe_ref[2*p]=jnp.where(low,qp,0.0).astype(bf16)
        qe_ref[2*p+1]=jnp.where(low,0.0,qp).astype(bf16)
    k_ref[...]=nn(n1,wk_ref[...]).astype(bf16)
    v=nn(n1,wv_ref[...]); v_ref[...]=v.astype(bf16)
    for p in range(2):
        vp=v[:,128*p:128*p+128]
        vx_ref[2*p]=jnp.where(low,vp,1.0).astype(bf16)
        vx_ref[2*p+1]=jnp.where(low,1.0,vp).astype(bf16)
    def block(r,kr):
        laneq=lax.broadcasted_iota(jnp.int32,(r.size,128),1); lowq=laneq<64
        ss=[nt(qe_ref[h,r,:],k_ref[kr,128*(h//2):128*(h//2)+128]) for h in range(4)]
        for p in range(2):
            os=[]
            for j in range(2):
                h=2*p+j
                s=ss[h]
                m=jnp.max(s,axis=-1,keepdims=True)
                e=jnp.exp(s-m).astype(bf16)
                o=nn(e,vx_ref[h,kr,:])
                lse=m+jnp.log(o)
                own=lowq if j==0 else ~lowq
                base=64 if j==0 else 0
                h3=tuple(-t for t in terms(lse))
                qe_ref[h,r,:]=ext(own,qe_ref[h,r,:].astype(f32),laneq,base,h3)
                os.append(o)
            num=jnp.where(lowq,os[0],os[1])
            den=pltpu.roll(jnp.where(lowq,os[1],os[0]),64,1)
            att_ref[r,128*p:128*p+128]=(num/den).astype(bf16)
    long=bucket_ref[0]==1
    @pl.when(long)
    def _():
        def body(i,_):
            block(pl.ds(i*QB,QB),slice(None)); return 0
        lax.fori_loop(0,T//QB,body,0)
    @pl.when(jnp.logical_not(long))
    def _():
        def body(i,_):
            r=pl.ds(i*SHORT,SHORT)
            block(r,r); return 0
        lax.fori_loop(0,T//SHORT,body,0)

def attn_fwd(bucket,x,g,b,w,QB=256):
    T,D=x.shape; G=D//256
    return pl.pallas_call(
        functools.partial(fwd_kernel,QB),
        grid=(G,),
        in_specs=[pl.BlockSpec(memory_space=pltpu.SMEM),
          pl.BlockSpec((T,D),lambda i:(0,0)),pl.BlockSpec((1,D),lambda i:(0,0)),pl.BlockSpec((1,D),lambda i:(0,0)),
          pl.BlockSpec((D,256),lambda i:(0,i)),pl.BlockSpec((D,256),lambda i:(0,i+G)),pl.BlockSpec((D,256),lambda i:(0,i+2*G))],
        out_specs=[pl.BlockSpec((T,D),lambda i:(0,0)),pl.BlockSpec((4,T,128),lambda i:(i,0,0)),
          pl.BlockSpec((T,256),lambda i:(0,i)),pl.BlockSpec((T,256),lambda i:(0,i)),pl.BlockSpec((T,256),lambda i:(0,i))],
        out_shape=[jax.ShapeDtypeStruct((T,D),bf16),jax.ShapeDtypeStruct((D//64,T,128),bf16)]+[jax.ShapeDtypeStruct((T,D),bf16)]*3,
        scratch_shapes=[pltpu.VMEM((4,T,128),bf16)],
        compiler_params=pltpu.CompilerParams(vmem_limit_bytes=48<<20),
        name="attn_fwd",
    )(bucket,x,g,b,w,w,w)

def bwd_kernel(KB,bucket_ref,qe_ref,k_ref,v_ref,att_ref,do_ref,dq_ref,dk_ref,dv_ref,doe_ref,ke_ref,ve_ref,dqa_ref):
    T=k_ref.shape[0]
    lane=lax.broadcasted_iota(jnp.int32,(T,128),1); low=lane<64
    do=do_ref[...].astype(f32)
    prod=do*att_ref[...].astype(f32)
    k=k_ref[...].astype(f32); v=v_ref[...].astype(f32)
    one0=jnp.where(lane<67,1.0,0.0); one1=jnp.where(lane<3,1.0,0.0)
    for j in range(2):
        own=low if j==0 else ~low
        d=jnp.sum(jnp.where(own,prod,0.0),axis=-1,keepdims=True)
        doe_ref[j]=ext(own,do,lane,64 if j==0 else 0,tuple(-t for t in terms(d)))
        ke_ref[j]=jnp.where(own,k,one0 if j==0 else one1).astype(bf16)
        ve_ref[j]=jnp.where(own,v,one0 if j==0 else one1).astype(bf16)
    def block(kr,qr,first):
        lowk=lax.broadcasted_iota(jnp.int32,(kr.size,128),1)<64
        dks=[];dvs=[];dqs=[]
        sts=[nt(ke_ref[j,kr,:],qe_ref[j,qr,:]) for j in range(2)]
        dpts=[nt(ve_ref[j,kr,:],doe_ref[j,qr,:]) for j in range(2)]
        for j in range(2):
            pt=jnp.exp(sts[j])
            ds=(pt*dpts[j]).astype(bf16)
            dvs.append(nn(pt.astype(bf16),do_ref[qr,:]))
            dks.append(nn(ds,qe_ref[j,qr,:]))
            dqs.append(tn(ds,k_ref[kr,:]))
        dk_ref[kr,:]=jnp.where(lowk,dks[0],dks[1]).astype(bf16)
        dv_ref[kr,:]=jnp.where(lowk,dvs[0],dvs[1]).astype(bf16)
        return dqs
    long=bucket_ref[0]==1
    @pl.when(long)
    def _():
        dqa_ref[...]=jnp.zeros_like(dqa_ref)
        def body(i,_):
            dqs=block(pl.ds(i*KB,KB),slice(None),True)
            dqa_ref[...]+=jnp.where(low,dqs[0],dqs[1])
            return 0
        lax.fori_loop(0,T//KB,body,0)
        dq_ref[...]=(dqa_ref[...]*0.125).astype(bf16)
    @pl.when(jnp.logical_not(long))
    def _():
        lows=lax.broadcasted_iota(jnp.int32,(SHORT,128),1)<64
        def body(i,_):
            r=pl.ds(i*SHORT,SHORT)
            dqs=block(r,r,True)
            dq_ref[r,:]=(jnp.where(lows,dqs[0],dqs[1])*0.125).astype(bf16)
            return 0
        lax.fori_loop(0,T//SHORT,body,0)

def attn_bwd(bucket,qe,k,v,att,do,KB=256):
    T,D=k.shape
    col=pl.BlockSpec((T,128),lambda i:(0,i))
    return pl.pallas_call(
        functools.partial(bwd_kernel,KB),
        grid=(D//128,),
        in_specs=[pl.BlockSpec(memory_space=pltpu.SMEM),pl.BlockSpec((2,T,128),lambda i:(i,0,0)),col,col,col,col],
        out_specs=[col]*3,
        out_shape=[jax.ShapeDtypeStruct((T,D),bf16)]*3,
        scratch_shapes=[pltpu.VMEM((2,T,128),bf16)]*3+[pltpu.VMEM((T,128),f32)],
        compiler_params=pltpu.CompilerParams(vmem_limit_bytes=48<<20),
        name="attn_bwd",
    )(bucket,qe,k,v,att,do)

ERF_P=0.43999999999999995*2**-0.5
ERF_C=(0.24822094504462977,0.24887131426512357,0.21731271244932707,0.215814984889486,-0.020185789068163502,0.2966929213019595,-0.2779510917809505,0.07122418451404043)
RPI=(2*3.141592653589793)**-0.5
def gelu_pair(u):
    t=1.0/(1.0+ERF_P*jnp.abs(u))
    e=jnp.exp(-0.5*(u*u))
    q=ERF_C[7]
    for c in ERF_C[6::-1]: q=q*t+c
    tail=(0.5*t)*q*e
    cdf=jnp.where(u>=0,1.0-tail,tail)
    return u*cdf, cdf+u*(e*RPI)

def mlp_kernel(RB,x_ref,att_ref,dy_ref,wo_ref,g_ref,b_ref,wu_ref,wd_ref,
               mid_ref,n2t_ref,mix_ref,gn2_ref,gwu_ref,gwd_ref,n2_ref,macc_ref,act_ref,gup_ref):
    j=pl.program_id(0); T=x_ref.shape[0]
    @pl.when(j==0)
    def _():
        def body(i,_):
            r=pl.ds(i*RB,RB)
            mid=x_ref[r,:].astype(f32)+nn(att_ref[r,:],wo_ref[...])
            mid_ref[r,:]=mid; macc_ref[r,:]=mid
            n2_ref[r,:]=ln_rows(mid,g_ref[...],b_ref[...]).astype(bf16)
            return 0
        lax.fori_loop(0,T//RB,body,0)
        n2t_ref[...]=n2_ref[...].T
        gn2_ref[...]=jnp.zeros_like(gn2_ref)
    def body(i,_):
        r=pl.ds(i*RB,RB)
        up=nn(n2_ref[r,:],wu_ref[...])
        da=nt(dy_ref[r,:],wd_ref[...])
        act,gp=gelu_pair(up)
        act=act.astype(bf16); gup=(da*gp).astype(bf16)
        act_ref[r,:]=act; gup_ref[r,:]=gup
        macc_ref[r,:]+=nn(act,wd_ref[...])
        gn2_ref[r,:]+=nt(gup,wu_ref[...])
        return 0
    lax.fori_loop(0,T//RB,body,0)
    gwd_ref[...]=tn(act_ref[...],dy_ref[...]).astype(bf16)
    gwu_ref[...]=nn(n2t_ref[...],gup_ref[...]).astype(bf16)
    @pl.when(j==pl.num_programs(0)-1)
    def _():
        mix_ref[...]=macc_ref[...].astype(bf16)

def mlp(x,att,dy,wo,g,b,wu,wd,FB=512,RB=512):
    T,D=x.shape; F=wu.shape[1]
    full=lambda s: pl.BlockSpec(s,lambda i:(0,)*len(s))
    return pl.pallas_call(functools.partial(mlp_kernel,RB),grid=(F//FB,),
      in_specs=[full((T,D)),full((T,D)),full((T,D)),full((D,D)),full((1,D)),full((1,D)),pl.BlockSpec((D,FB),lambda i:(0,i)),pl.BlockSpec((FB,D),lambda i:(i,0))],
      out_specs=[full((T,D)),full((D,T)),full((T,D)),full((T,D)),pl.BlockSpec((D,FB),lambda i:(0,i)),pl.BlockSpec((FB,D),lambda i:(i,0))],
      out_shape=[jax.ShapeDtypeStruct((T,D),f32),jax.ShapeDtypeStruct((D,T),bf16),jax.ShapeDtypeStruct((T,D),bf16),jax.ShapeDtypeStruct((T,D),f32),
        jax.ShapeDtypeStruct((D,F),bf16),jax.ShapeDtypeStruct((F,D),bf16)],
      scratch_shapes=[pltpu.VMEM((T,D),bf16),pltpu.VMEM((T,D),f32),pltpu.VMEM((T,FB),bf16),pltpu.VMEM((T,FB),bf16)],
      compiler_params=pltpu.CompilerParams(vmem_limit_bytes=56<<20),name="mlp")(x,att,dy,wo,g,b,wu,wd)

def ln_back(gn,v,gain):
    mu=jnp.mean(v,axis=-1,keepdims=True); c=v-mu
    r=lax.rsqrt(jnp.mean(c*c,axis=-1,keepdims=True)+LN_EPS); xh=c*r
    gg=gn*gain
    dx=r*(gg-jnp.mean(gg,axis=-1,keepdims=True)-xh*jnp.mean(gg*xh,axis=-1,keepdims=True))
    return dx, jnp.sum(gn*xh,axis=0,keepdims=True), jnp.sum(gn,axis=0,keepdims=True)

def mid_kernel(gn2_ref,mid_ref,dy_ref,att_ref,wo_ref,g_ref,gmid_ref,gatt_ref,gwo_ref,gg_ref,gb_ref,gm_ref):
    T=dy_ref.shape[0]; RB=256
    gg_ref[...]=jnp.zeros_like(gg_ref); gb_ref[...]=jnp.zeros_like(gb_ref)
    def body(i,_):
        r=pl.ds(i*RB,RB)
        dx,dg,db=ln_back(gn2_ref[r,:],mid_ref[r,:],g_ref[...])
        gm=dy_ref[r,:].astype(f32)+dx
        gmid_ref[r,:]=gm; gmb=gm.astype(bf16); gm_ref[r,:]=gmb
        gg_ref[...]+=dg; gb_ref[...]+=db
        gatt_ref[r,:]=nt(gmb,wo_ref[...]).astype(bf16)
        return 0
    lax.fori_loop(0,T//RB,body,0)
    gwo_ref[...]=tn(att_ref[...],gm_ref[...]).astype(bf16)
def midk(gn2,mid,dy,att,wo,g):
    T,D=dy.shape
    return pl.pallas_call(mid_kernel,out_shape=[jax.ShapeDtypeStruct((T,D),f32),jax.ShapeDtypeStruct((T,D),bf16),jax.ShapeDtypeStruct((D,D),bf16),jax.ShapeDtypeStruct((1,D),f32),jax.ShapeDtypeStruct((1,D),f32)],
      scratch_shapes=[pltpu.VMEM((T,D),bf16)],compiler_params=pltpu.CompilerParams(vmem_limit_bytes=48<<20),name="midk")(gn2,mid,dy,att,wo,g)

def wq_kernel(n1_ref,dq_ref,dk_ref,dv_ref,gw_ref):
    n1t=n1_ref[...].T
    for i,d in enumerate((dq_ref,dk_ref,dv_ref)):
        gw_ref[i]=nn(n1t,d[...]).astype(bf16)
def wqk(n1,dq,dk,dv):
    T,D=n1.shape
    return pl.pallas_call(wq_kernel,out_shape=jax.ShapeDtypeStruct((3,D,D),bf16),compiler_params=pltpu.CompilerParams(vmem_limit_bytes=48<<20),name="wqk")(n1,dq,dk,dv)

def tail_kernel(x_ref,dq_ref,dk_ref,dv_ref,w_ref,gmid_ref,g_ref,tg_ref,gg_ref,gb_ref):
    T,D=x_ref.shape; RB=256
    gg_ref[...]=jnp.zeros_like(gg_ref); gb_ref[...]=jnp.zeros_like(gb_ref)
    def body(i,_):
        r=pl.ds(i*RB,RB)
        gn=nt(dq_ref[r,:],w_ref[:,:D])+nt(dk_ref[r,:],w_ref[:,D:2*D])+nt(dv_ref[r,:],w_ref[:,2*D:])
        dx,dg,db=ln_back(gn,x_ref[r,:].astype(f32),g_ref[...])
        tg_ref[r,:]=(gmid_ref[r,:]+dx).astype(bf16)
        gg_ref[...]+=dg; gb_ref[...]+=db
        return 0
    lax.fori_loop(0,T//RB,body,0)
def tailk(x,dq,dk,dv,w,gmid,g):
    T,D=x.shape
    return pl.pallas_call(tail_kernel,out_shape=[jax.ShapeDtypeStruct((T,D),bf16),jax.ShapeDtypeStruct((1,D),f32),jax.ShapeDtypeStruct((1,D),f32)],
      compiler_params=pltpu.CompilerParams(vmem_limit_bytes=48<<20),name="tailk")(x,dq,dk,dv,w,gmid,g)


def gather(v):
    return lax.all_gather(v, "fsdp", axis=0, tiled=True)


def scatter_sum(v):
    part = lax.psum_scatter(v.astype(bf16), "fsdp", scatter_dimension=0, tiled=True)
    return lax.psum(part, "rep").astype(f32)


def shards(tokens, bucket, ln1_gain, ln1_bias, w_qkv, w_out, ln2_gain, ln2_bias, w_up, w_down, cotangent):
    width = tokens.shape[1]
    norms = lax.all_gather(jnp.stack([ln1_gain, ln1_bias, ln2_gain, ln2_bias]), "fsdp", axis=1, tiled=True).astype(f32)
    gain_one, bias_one, gain_two, bias_two = (norms[i : i + 1] for i in range(4))
    full_qkv, full_out, full_up, full_down = (gather(w) for w in (w_qkv, w_out, w_up, w_down))
    normed_one, q_ext, keys, values, attended = attn_fwd(bucket, tokens, gain_one, bias_one, full_qkv)
    middle, _, mixed, grad_n2, gw_up, gw_down = mlp(
        tokens, attended, cotangent, full_out, gain_two, bias_two, full_up, full_down
    )
    grad_mid, grad_att, gw_out, g_gain2, g_bias2 = midk(grad_n2, middle, cotangent, attended, full_out, gain_two)
    gq, gk, gv = attn_bwd(bucket, q_ext, keys, values, attended, grad_att)
    gw_qkv = wqk(normed_one, gq, gk, gv)
    tokens_grad, g_gain1, g_bias1 = tailk(tokens, gq, gk, gv, full_qkv, grad_mid, gain_one)
    g_norms = jnp.concatenate([g_gain1, g_bias1, g_gain2, g_bias2], axis=0)
    g_norms = lax.psum(lax.psum_scatter(g_norms, "fsdp", scatter_dimension=1, tiled=True), "rep")
    return (
        mixed,
        tokens_grad,
        g_norms[0],
        g_norms[1],
        scatter_sum(gw_qkv.transpose(1, 0, 2).reshape(width, 3 * width)),
        scatter_sum(gw_out),
        g_norms[2],
        g_norms[3],
        scatter_sum(gw_up),
        scatter_sum(gw_down),
    )


def solution(mesh):
    return jax.shard_map(
        shards,
        mesh=mesh,
        in_specs=(
            P(("rep", "fsdp"), None),
            P(("rep", "fsdp")),
            P("fsdp"),
            P("fsdp"),
            P("fsdp", None),
            P("fsdp", None),
            P("fsdp"),
            P("fsdp"),
            P("fsdp", None),
            P("fsdp", None),
            P(("rep", "fsdp"), None),
        ),
        out_specs=(
            P(("rep", "fsdp"), None),
            P(("rep", "fsdp"), None),
            P("fsdp"),
            P("fsdp"),
            P("fsdp", None),
            P("fsdp", None),
            P("fsdp"),
            P("fsdp"),
            P("fsdp", None),
            P("fsdp", None),
        ),
        check_vma=False,
    )
```

time: 702 us -> 622 us (0.89); the launches traced: 692 us -> 621 us
  matrix products: 289 us -> 0 us
  waiting for transfers between devices: 167 us -> 401 us
  Pallas kernels: 0 us -> 153 us
  other arithmetic: 99.3 us -> 2.97 us
  local copies, waits for them, and re-layouts: 67.1 us -> 26.1 us
  blocking collectives: 41.4 us -> 22.2 us
  loops' own time: 11.8 us -> 0 us
    dot_general x26 -> x0, matrix products: 289 us -> none  [the longest x4 44.8 us: block_scores(): jnp.einsum('qhd,khd->hqk', query_blk, keys_all, preferred_element_type=jn...]
    pallas_call x0 -> x6, Pallas kernels: none -> 153 us  [the longest x1 52.2 us: mlp(): pl.pallas_call(functools.partial(mlp_kernel, RB), grid=(F // FB,), in_spe...]
    all_gather x4, waiting for transfers between devices: 9.28 us -> 102 us  [gather(): return lax.all_gather(v, 'fsdp', axis=0, tiled=True)]
    unnamed x9 -> x12, waiting for transfers between devices: 2.66 us -> 74.6 us
    convert_element_type x16 -> x4, other arithmetic: 58.8 us -> 2.94 us  [the longest x3 2.94 us: scatter_sum(): return lax.psum(part, 'rep').astype(f32)]
    reduce_scatter x4 -> x3, waiting for transfers between devices: 115 us -> 154 us  [scatter_sum(): lax.psum_scatter(v.astype(bf16), 'fsdp', scatter_dimension=0, tiled=True)]
    reduce_sum x9 -> x0, other arithmetic: 35.7 us -> none  [the longest x2 25.4 us: forward_block(): total = jnp.sum(expo, axis=-1, keepdims=True)]
    psum x1, waiting for transfers between devices: 39.3 us -> 71.8 us  [scatter_sum(): return lax.psum(part, 'rep').astype(f32)]
  transfers between devices with their start and end apart: 9 -> 10, of which waited for: 5 -> 9; matrix products, arithmetic and copies ran while one was open for 55% -> 1% of each run, Pallas kernels for 0% -> 6%
where the time goes in v1:
time: 622 us; the launch traced here: 621 us
  waiting for transfers between devices  401 us (64%)
  Pallas kernels  153 us (25%)
  local copies, waits for them, and re-layouts  26.1 us (4%)
  blocking collectives  22.2 us (4%)
  between operations  15 us (2%)
    reduce_scatter x3, waiting for transfers between devices, scatter_sum(): lax.psum_scatter(v.astype(bf16), 'fsdp', scatter_dimension=0, tiled=True)  154 us
    all_gather x4, waiting for transfers between devices, gather(): return lax.all_gather(v, 'fsdp', axis=0, tiled=True)  102 us
    unnamed x12, waiting for transfers between devices  74.6 us
    psum x1, waiting for transfers between devices, scatter_sum(): return lax.psum(part, 'rep').astype(f32)  71.8 us
    pallas_call x1, Pallas kernels, mlp(): pl.pallas_call(functools.partial(mlp_kernel, RB), grid=(F // FB,), in_spe...  52.2 us
    pallas_call x1, Pallas kernels, attn_bwd(): pl.pallas_call(functools.partial(bwd_kernel, KB), grid=(D // 128,), in_sp...  44.8 us
    pallas_call x1, Pallas kernels, attn_fwd(): pl.pallas_call(functools.partial(fwd_kernel, QB), grid=(G,), in_specs=[pl...  28.5 us
    unnamed x39, local copies, waits for them, and re-layouts  18.8 us
  transfers between devices with their start and end apart: 10, of which 9 were waited for; matrix products, arithmetic and copies ran while one was open for 1% of the time, Pallas kernels for 6%

profile of v1, /device:TPU:0, one launch (start us, length us, event | category | flops | bytes accessed | tf_op | source)
XLA Modules:
  0.0 621.5 jit_solution(17436560210018986139)
XLA Ops:
  7.3 0.7 all-gather.6.cloned.1.call-update
  8.0 0.0 all-gather.8.cloned.1.call-start
  8.0 0.7 all-gather.8.cloned.1.call-update
  8.7 0.0 all-gather.10.cloned.1.call-start
  8.7 0.7 all-gather.10.cloned.1.call-update
  9.5 0.5 all-gather.12.cloned.1.call-update
  10.0 0.0 reduce-scatter.18.cloned.1.call-start
  10.8 10.3 %all-gather = bf16[8,96,4]{1,2,0:T(4,128)(2,1)S(1)} all-gather(bf16[1,96,4]{1,2,0:T(4,128)(2,1)S(1)} %maximum_bitcast_fusion), channel_id=1, replica_groups=mesh['rep'=4,'fsdp'=8] {'fsdp'}, dimensions={0}, use_global_device_ids=true | all-gather | bytes 6912 | tf_op jit(solution)/shard_map/all_gather | solution.py:278
  21.1 0.1 reshape.26
  21.2 0.6 fusion
  21.8 24.8 %all-gather.6.cloned.1.call-done.wq_ref.wk_ref.wv_ref.w_ref = bf16[768,2304]{1,0:T(8,128)(2,1)} async-done(((bf16[96,2304]{1,0:T(8,128)(2,1)}), bf16[768,2304]{1,0:T(8,128)(2,1)}) %all-gather.6.cloned.1.call-update) | async-done | bytes 3538960 | tf_op jit(solution)/shard_map/all_gather | solution.py:268
  46.6 28.5 %attn_fwd.1 = (bf16[1024,768]{1,0:T(8,128)(2,1)S(1)}, bf16[12,1024,128]{2,1,0:T(8,128)(2,1)}, bf16[1024,768]{1,0:T(8,128)(2,1)S(1)}, bf16[1024,768]{1,0:T(8,128)(2,1)S(1)}, bf16[1024,768]{1,0:T(8,128)(2,1)}) custom-call(s32[1]{0:T(128)S(6)} %copy.40.bucket_ref, bf16[1024,768]{1,0:T(8,128)(2,1)} %x_ref.5, f32[1,768]{1,0:T(1,128)S(1)} %get-tuple-element.89.g_ref, ...), custom_call_target="tpu_custom_call" | custom-call | tf_op jit(solution)/shard_map/attn_fwd/pallas_call | solution.py:88
  75.1 1.1 copy-done.6
  76.3 1.2 copy-done.7
  77.4 36.0 %all-gather.10.cloned.1.call-done.wu_ref = bf16[768,3072]{1,0:T(8,128)(2,1)} async-done(((bf16[96,3072]{1,0:T(8,128)(2,1)}), bf16[768,3072]{1,0:T(8,128)(2,1)}) %all-gather.10.cloned.1.call-update) | async-done | bytes 4718608 | tf_op jit(solution)/shard_map/all_gather | solution.py:268
  113.5 40.7 %all-gather.12.cloned.1.call-done.wd_ref = bf16[3072,768]{1,0:T(8,128)(2,1)} async-done(((bf16[384,768]{1,0:T(8,128)(2,1)}), bf16[3072,768]{1,0:T(8,128)(2,1)}) %all-gather.12.cloned.1.call-update) | async-done | bytes 4718608 | tf_op jit(solution)/shard_map/all_gather | solution.py:268
  154.2 52.2 %mlp.1 = (f32[1024,768]{1,0:T(8,128)}, bf16[768,1024]{1,0:T(8,128)(2,1)}, bf16[1024,768]{1,0:T(8,128)(2,1)}, f32[1024,768]{1,0:T(8,128)}, bf16[768,3072]{1,0:T(8,128)(2,1)}, /*index=5*/bf16[3072,768]{1,0:T(8,128)(2,1)}) custom-call(bf16[1024,768]{1,0:T(8,128)(2,1)} %x_ref.5, bf16[1024,768]{1,0:T(8,128)(2,1)} %get-tuple-element.31.att_ref, ...), custom_call_target="tpu_custom_call" | custom-call | tf_op jit(solution)/shard_map/mlp/pallas_call | solution.py:209
  206.4 9.6 %midk.1 = (f32[1024,768]{1,0:T(8,128)}, bf16[1024,768]{1,0:T(8,128)(2,1)S(1)}, bf16[768,768]{1,0:T(8,128)(2,1)}, f32[1,768]{1,0:T(1,128)S(1)}, f32[1,768]{1,0:T(1,128)S(1)}) custom-call(f32[1024,768]{1,0:T(8,128)} %get-tuple-element.36.gn2_ref, f32[1024,768]{1,0:T(8,128)} %get-tuple-element.37.mid_ref, bf16[1024,768]{1,0:T(8,128)(2,1)S(1)} %copy-done.1, ...), custom_call_target="tpu_custom_call" | custom-call | tf_op jit(solution)/shard_map/midk/pallas_call | solution.py:239
  216.0 1.2 copy-done.8
  217.3 44.8 %attn_bwd.1 = (bf16[1024,768]{1,0:T(8,128)(2,1)S(1)}, bf16[1024,768]{1,0:T(8,128)(2,1)S(1)}, bf16[1024,768]{1,0:T(8,128)(2,1)S(1)}) custom-call(s32[1]{0:T(128)S(6)} %copy.40.bucket_ref, bf16[12,1024,128]{2,1,0:T(8,128)(2,1)} %get-tuple-element.33.qe_ref, bf16[1024,768]{1,0:T(8,128)(2,1)} %copy-done.6, bf16[1024,768]{1,0:T(8,128)(2,1)} %copy-done.7, ...), custom_call_target="tpu_custom_call" | custom-call | tf_op jit(solution)/shard_map/attn_bwd/pallas_call | solution.py:152
  262.0 1.2 copy-done.4
  263.2 7.7 %wqk.1 = bf16[3,768,768]{2,1,0:T(8,128)(2,1)} custom-call(bf16[1024,768]{1,0:T(8,128)(2,1)S(1)} %get-tuple-element.48.n1_ref, bf16[1024,768]{1,0:T(8,128)(2,1)S(1)} %get-tuple-element.39.dq_ref, bf16[1024,768]{1,0:T(8,128)(2,1)S(1)} %get-tuple-element.40.dk_ref, bf16[1024,768]{1,0:T(8,128)(2,1)} %copy-done.4), custom_call_target="tpu_custom_call" | custom-call | tf_op jit(solution)/shard_map/wqk/pallas_call | solution.py:248
  270.9 6.0 copy.29
  277.0 5.8 copy.33
  282.8 0.0 reduce-scatter.10.cloned.1.call-start
  282.8 0.5 reduce-scatter.10.cloned.1.call-update
  283.4 0.7 reduce-scatter.12.cloned.1.call-update
  284.2 0.7 reduce-scatter.14.cloned.1.call-update
  284.9 0.0 reduce-scatter.16.cloned.1.call-start
  284.9 0.7 copy-done
  285.6 1.4 copy-done.3
  287.0 10.7 %tailk.1 = (bf16[1024,768]{1,0:T(8,128)(2,1)}, f32[1,768]{1,0:T(1,128)S(1)}, f32[1,768]{1,0:T(1,128)S(1)}) custom-call(bf16[1024,768]{1,0:T(8,128)(2,1)S(1)} %copy-done, bf16[1024,768]{1,0:T(8,128)(2,1)S(1)} %get-tuple-element.39.dq_ref, bf16[1024,768]{1,0:T(8,128)(2,1)S(1)} %copy-done.3, bf16[1024,768]{1,0:T(8,128)(2,1)} %copy-done.4, ...), custom_call_target="tpu_custom_call" | custom-call | tf_op jit(solution)/shard_map/tailk/pallas_call | solution.py:263
  297.7 0.9 copy.31
  298.6 0.0 all-reduce.3.cloned.1.call-start
  298.7 32.3 %reduce-scatter.18.cloned.1.call-done = bf16[96,2304]{1,0:T(8,128)(2,1)} async-done(((bf16[768,2304]{1,0:T(8,128)(2,1)}), bf16[96,2304]{1,0:T(8,128)(2,1)}) %reduce-scatter.18.cloned.1.call-update) | async-done | bytes 442384
  331.0 2.1 copy.34
  333.1 38.4 %reduce-scatter.10.cloned.1.call-done = bf16[96,768]{1,0:T(8,128)(2,1)} async-done(((bf16[768,768]{1,0:T(8,128)(2,1)}), bf16[96,768]{1,0:T(8,128)(2,1)}) %reduce-scatter.10.cloned.1.call-update) | async-done | bytes 147472 | tf_op jit(solution)/shard_map/reduce_scatter | solution.py:272
  371.5 57.7 %reduce-scatter.12.cloned.1.call-done = bf16[96,3072]{1,0:T(8,128)(2,1)} async-done(((bf16[768,3072]{1,0:T(8,128)(2,1)}), bf16[96,3072]{1,0:T(8,128)(2,1)}) %reduce-scatter.12.cloned.1.call-update) | async-done | bytes 589840 | tf_op jit(solution)/shard_map/reduce_scatter | solution.py:272
  429.2 57.4 %reduce-scatter.14.cloned.1.call-done = bf16[384,768]{1,0:T(8,128)(2,1)} async-done(((bf16[3072,768]{1,0:T(8,128)(2,1)}), bf16[384,768]{1,0:T(8,128)(2,1)}) %reduce-scatter.14.cloned.1.call-update) | async-done | bytes 589840 | tf_op jit(solution)/shard_map/reduce_scatter | solution.py:272
  486.6 37.8 %reduce-scatter.16.cloned.1.call-done = f32[96,4]{1,0:T(8,128)} async-done(((f32[768,4]{1,0:T(8,128)}), f32[96,4]{1,0:T(8,128)}) %reduce-scatter.16.cloned.1.call-update) | async-done | bytes 1552
  524.4 0.9 copy.32
  525.2 11.8 %psum.35 = f32[4,96]{1,0:T(4,128)S(1)} all-reduce(f32[4,96]{1,0:T(4,128)S(1)} %copy.32), channel_id=1, replica_groups=mesh['rep'=4,'fsdp'=8] {'rep'}, use_global_device_ids=true, to_apply=%region_1.0 | all-reduce | flops 384 | bytes 3072 | tf_op jit(solution)/shard_map/psum | solution.py:290
  537.1 0.5 slice_bitcast_fusion
  537.6 71.8 %all-reduce.3.cloned.1.call-done = (bf16[96,2304]{0,1:T(8,128)(2,1)}, bf16[96,768]{1,0:T(8,128)(2,1)}, bf16[96,3072]{1,0:T(8,128)(2,1)}, bf16[384,768]{1,0:T(8,128)(2,1)}) async-done(((bf16[96,2304]{0,1:T(8,128)(2,1)}, bf16[96,768]{1,0:T(8,128)(2,1)}, bf16[96,3072]{1,0:T(8,128)(2,1)}, bf16[384,768]{1,0:T(8,128)(2,1)}), (bf16[96,2304]{0,1:T(8,128)(2,1)}, bf16[96,768]{1,0:T(8,128)(2,1)}, ...) | async-done | bytes 1769488 | tf_op jit(solution)/shard_map/psum | solution.py:273
  609.4 2.3 copy.30
  611.7 0.7 convert_element_type.17
  612.4 1.1 convert_element_type.18
  613.6 1.1 convert_element_type.19
  (39 shorter events, 0.3 us)
Async XLA Ops:
  7.2 3.5 copy-start.13
  7.2 3.5 copy-start.14
  7.2 3.5 copy-start.15
  7.2 3.5 copy-start.16
  7.2 39.4 %all-gather.6.cloned.1.call-start = ((), (), s32[]{:S(2)}) async-start(), calls=%async_computation.5 | async-start | bytes 3981312 | tf_op jit(solution)/shard_map/all_gather | solution.py:268
  8.0 69.5 %all-gather.8.cloned.1.call-start = ((), (), s32[]{:S(2)}) async-start(), calls=%async_computation.6 | async-start | bytes 1327104 | tf_op jit(solution)/shard_map/all_gather | solution.py:268
  8.7 104.8 %all-gather.10.cloned.1.call-start = ((), (), s32[]{:S(2)}) async-start(), calls=%async_computation.7 | async-start | bytes 5308416 | tf_op jit(solution)/shard_map/all_gather | solution.py:268
  9.4 144.7 %all-gather.12.cloned.1.call-start = ((), (), s32[]{:S(2)}) async-start(), calls=%async_computation.8 | async-start | bytes 5308416 | tf_op jit(solution)/shard_map/all_gather | solution.py:268
  10.0 321.0 %reduce-scatter.18.cloned.1.call-start = ((), (), s32[]{:S(2)}) async-start(), calls=%async_computation.13 | async-start | bytes 3981312
  75.1 1.1 copy-start.6
  76.3 1.2 copy-start.7
  154.2 52.3 %copy-start.1 = (bf16[1024,768]{1,0:T(8,128)(2,1)S(1)}, bf16[1024,768]{1,0:T(8,128)(2,1)}, u32[]{:S(2)}) copy-start(bf16[1024,768]{1,0:T(8,128)(2,1)} %dy_ref.3) | copy-start | bytes 4718596
  154.2 52.3 %copy-start.5 = (bf16[768,768]{1,0:T(8,128)(2,1)S(1)}, bf16[768,768]{1,0:T(8,128)(2,1)}, u32[]{:S(2)}) copy-start(bf16[768,768]{1,0:T(8,128)(2,1)} %all-gather.8.cloned.1.call-done.wo_ref) | copy-start | bytes 3538948
  154.2 52.3 %copy-start.9 = (f32[1,768]{1,0:T(1,128)S(1)}, f32[1,768]{1,0:T(1,128)}, u32[]{:S(2)}) copy-start(f32[1,768]{1,0:T(1,128)} %get-tuple-element.87.g_ref) | copy-start | bytes 9220
  216.0 1.2 copy-start.8
  262.0 1.2 copy-start.4
  263.2 7.7 %copy-start.2 = (bf16[1024,768]{1,0:T(8,128)(2,1)}, bf16[1024,768]{1,0:T(8,128)(2,1)S(1)}, u32[]{:S(2)}) copy-start(bf16[1024,768]{1,0:T(8,128)(2,1)S(1)} %get-tuple-element.40.dk_ref) | copy-start | bytes 4718596
  282.8 88.7 %reduce-scatter.10.cloned.1.call-start = ((), (), s32[]{:S(2)}) async-start(), calls=%async_computation.9 | async-start | bytes 1327104 | tf_op jit(solution)/shard_map/reduce_scatter | solution.py:272
  283.4 145.9 %reduce-scatter.12.cloned.1.call-start = ((), (), s32[]{:S(2)}) async-start(), calls=%async_computation.10 | async-start | bytes 5308416 | tf_op jit(solution)/shard_map/reduce_scatter | solution.py:272
  284.1 202.5 %reduce-scatter.14.cloned.1.call-start = ((), (), s32[]{:S(2)}) async-start(), calls=%async_computation.11 | async-start | bytes 5308416 | tf_op jit(solution)/shard_map/reduce_scatter | solution.py:272
  284.2 1.4 copy-start
  284.9 239.5 %reduce-scatter.16.cloned.1.call-start = ((), (), s32[]{:S(2)}) async-start(), calls=%async_computation.12 | async-start | bytes 442368
  285.6 1.4 copy-start.3
  298.6 310.7 %all-reduce.3.cloned.1.call-start = ((), (), s32[]{:S(2)}) async-start(), calls=%async_computation.14 | async-start | bytes 3833856 | tf_op jit(solution)/shard_map/psum | solution.py:273
  609.4 2.3 copy-start.12
  609.4 3.1 copy-start.11
  609.4 4.2 copy-start.10
Sparse Core Ops, SparseCore 0:
  9.9 36.6 all-gather.5
  48.5 24.0 all-gather.7
  74.5 38.9 all-gather.9
  115.2 38.9 all-gather.11
  282.9 48.0 reduce-scatter.17
  334.7 36.7 reduce-scatter.9
  375.3 53.8 reduce-scatter.11
  432.7 53.8 reduce-scatter.13
  490.5 33.8 reduce-scatter.15
  527.6 81.6 all-reduce.2
